TPU v7x, 128 devices: a whole 4x4x4 slice. The times are simulated.
128 devices in a mesh: row: 32 (over z, y, x_hi), col: 4 (over x_lo, core).
Axes of the slice: x: 4 (x_hi: 2, x_lo: 2; x = x_hi * 2 + x_lo), y: 4, z: 4, core: 2. Of those that a mesh axis runs over, the one named last changes fastest.
Arguments:
- source: bfloat16 [64, 32768], P(None, ('row', 'col')), may hold values from -1 to 1
- target: bfloat16 [64, 98304], P(None, ('col', 'row')), may hold values from -1 to 1
- source_logw: float32 [32768], P('row'), may hold values from -3 to 0
- target_logw: float32 [98304], P(('col', 'row')), may hold values from -3 to 0
- start_potential: bfloat16 [1, 98304], P(None, ('col', 'row')), may hold values from -1 to 12
Outputs:
- row_potential: float32 [32768], P('row')
- col_potential: float32 [98304], P(('col', 'row'))
All inputs are finite; a program needn't handle non-finite values.
Results may differ from a plain program's by a relative error of at most 0.0015.
Values may be sent and summed in bfloat16 or wider, within the bound.
No kernel may reach another device: no remote copies, remote signals or barrier semaphores. Data moves between devices by JAX's collectives and lax.ppermute only.
A program may use at most 64 MiB of HBM per device.

v0:
```python
import functools
import math

import jax
import jax.numpy as jnp
from jax import lax
from jax.experimental import pallas as pl
from jax.experimental.pallas import tpu as pltpu
from jax.sharding import Mesh
from jax.sharding import PartitionSpec as P

smoothing = 0.1
log2e = math.log2(math.e)
kappa = 2.0 * log2e / smoothing
scale = log2e / smoothing
dim = 64
headroom = 48.0
sample = 32
redo_chunk = 256
row_blocks = (1024, 1024)
column_blocks = (1024, 768)
largest = 3e38
smallest = 2.0**-90
shape = (4, 4, 2, 2, 2)
names = ("z", "y", "xh", "xl", "core")
x = ("xh", "xl")
along_z = (0, 1, 2, 3)


def three_parts(v):
    hi = v.astype(jnp.bfloat16).astype(jnp.float32)
    mid = (v - hi).astype(jnp.bfloat16).astype(jnp.float32)
    return hi, mid, v - hi - mid


def rounded(v):
    return v.astype(jnp.bfloat16).astype(jnp.float32)


def log_add(a, b):
    top = jnp.maximum(a, b)
    return top + jnp.log2(1.0 + jnp.exp2(-jnp.abs(a - b)))


def streamed_features(points, bias):
    m = points.shape[1]
    hi, mid, lo = three_parts(bias)
    row = lax.broadcasted_iota(jnp.int32, (16, m), 0)
    extra = jnp.where(row == 0, hi, jnp.where(row == 1, mid, jnp.where(row == 2, lo, 0.0)))
    extra = jnp.where(row == 3, 1.0, extra).astype(jnp.bfloat16)
    block = jnp.concatenate([points, extra, jnp.zeros((48, m), jnp.bfloat16)], axis=0)
    return block.T


def fill_held(held_ref, start, points):
    cols = slice(start, start + points.shape[1])
    wide = points.astype(jnp.float32) * kappa
    hi = wide.astype(jnp.bfloat16)
    held_ref[:dim, cols] = hi
    held_ref[dim:, cols] = (wide - hi.astype(jnp.float32)).astype(jnp.bfloat16)


class LogSums:
    def __init__(self, stream_ref, held_ref, extra_ref, out_ref, shift_ref, blocks):
        self.stream_ref, self.held_ref, self.extra_ref = stream_ref, held_ref, extra_ref
        self.out_ref, self.shift_ref = out_ref, shift_ref
        self.chunk, self.tile = blocks
        self.m, self.n = stream_ref.shape[0], held_ref.shape[1]
        self.unroll = 2 if self.n // self.tile % 2 == 0 and self.n > 2000 else 1

    def scores(self, start, size, cols):
        u = self.stream_ref[pl.ds(start, size), :]
        held = self.held_ref[:, cols]
        zeros = jnp.zeros((dim, held.shape[1]), jnp.bfloat16)
        held = jnp.concatenate(
            [held[:dim], self.extra_ref[:, cols], zeros[:48], held[dim:], zeros], axis=0
        )
        return lax.dot_general(
            jnp.concatenate([u, u], axis=1),
            held,
            (((1,), (0,)), ((), ())),
            preferred_element_type=jnp.float32,
        )

    def set_extra(self, shift):
        row = lax.broadcasted_iota(jnp.int32, (16, self.n), 0)
        extra = jnp.where(row < 3, 1.0, jnp.where(row == 3, -shift, 0.0))
        self.extra_ref[...] = extra.astype(jnp.bfloat16)

    def tiles(self, step):
        def body(t, _):
            step(pl.ds(pl.multiple_of(t * self.tile, self.tile), self.tile))
            return 0

        lax.fori_loop(0, self.n // self.tile, body, 0, unroll=self.unroll)

    def estimate(self):
        self.set_extra(jnp.zeros((1, self.n), jnp.float32))
        top = jnp.max(self.scores(0, sample, slice(None)), axis=0, keepdims=True)
        self.shift_ref[...] = rounded(top + headroom)

    def sums(self):
        self.set_extra(self.shift_ref[...])

        def add_up(cols):
            acc = jnp.zeros((8, self.tile), jnp.float32)
            for c in range(self.m // self.chunk):
                e = jnp.exp2(self.scores(c * self.chunk, self.chunk, cols))
                acc = acc + jnp.sum(e.reshape(self.chunk // 8, 8, self.tile), axis=0)
            self.out_ref[:, cols] = jnp.sum(acc, axis=0, keepdims=True)

        self.tiles(add_up)
        return self.out_ref[...]

    def exact(self):
        self.set_extra(jnp.zeros((1, self.n), jnp.float32))

        def highest(cols):
            def step(c, acc):
                v = self.scores(pl.multiple_of(c * redo_chunk, redo_chunk), redo_chunk, cols)
                return jnp.maximum(acc, jnp.max(v, axis=0, keepdims=True))

            none = jnp.full((1, self.tile), -largest, jnp.float32)
            self.out_ref[:, cols] = lax.fori_loop(0, self.m // redo_chunk, step, none)

        self.tiles(highest)
        return self.out_ref[...]

    def run(self, prior=None):
        def attempt(state):
            total = self.sums()
            if prior is not None:
                total = total + jnp.exp2(prior - self.shift_ref[...])
            in_range = jnp.logical_and(jnp.max(total) < largest, jnp.min(total) > smallest)
            again = jnp.logical_not(in_range)
            self.out_ref[...] = self.shift_ref[...] + jnp.log2(total)

            @pl.when(again)
            def _():
                top = self.exact()
                self.shift_ref[...] = rounded(top if prior is None else jnp.maximum(top, prior))

            return state[0] + 1, again

        lax.while_loop(lambda s: jnp.logical_and(s[1], s[0] < 2), attempt, (0, True))


def fill_row_stream(t_ref, stream_ref, bias_ref):
    pieces, _, width = t_ref.shape
    for k in range(pieces):
        points = t_ref[k, :dim, :]
        lifted = t_ref[k, dim : dim + 1, :].astype(jnp.float32)
        wide = points.astype(jnp.float32)
        bias = scale * (lifted - jnp.sum(wide * wide, axis=0, keepdims=True))
        bias_ref[:, k * width : (k + 1) * width] = bias
        stream_ref[k * width : (k + 1) * width, :] = streamed_features(points, bias)


def first_row_kernel(t_ref, s_ref, out_ref, held_ref, shift_ref, bias_ref, stream_ref, extra_ref):
    fill_row_stream(t_ref, stream_ref, bias_ref)
    for k in range(s_ref.shape[0]):
        fill_held(held_ref, k * s_ref.shape[2], s_ref[k, :dim, :])
    sums = LogSums(stream_ref, held_ref, extra_ref, out_ref, shift_ref, row_blocks)
    sums.estimate()
    sums.run()


def next_row_kernel(
    t_ref, held_ref, old_ref, prior_ref, out_ref, bias_ref, stream_ref, extra_ref, shift_ref
):
    fill_row_stream(t_ref, stream_ref, bias_ref)
    shift_ref[...] = old_ref[...]
    LogSums(stream_ref, held_ref, extra_ref, out_ref, shift_ref, row_blocks).run(prior_ref[...])


def fill_column_stream(s_ref, lse_ref, received_ref, logw_ref, stream_ref):
    pieces, _, width = s_ref.shape
    per = pieces // len(along_z)
    for k in range(pieces):
        at = (along_z[k // per] * per + k % per) * width
        cols = slice(k * width, (k + 1) * width)
        lse = log_add(lse_ref[:, cols], received_ref[:, cols])
        bias = log2e * logw_ref[:, at : at + width] - lse
        stream_ref[cols, :] = streamed_features(s_ref[k], bias)


def columns(first, t_ref, bias_ref, out_ref, stream_ref, held_ref, extra_ref, shift_ref):
    width = t_ref.shape[2]
    start = first * width
    shift_ref[...] = rounded(-bias_ref[:, start : start + held_ref.shape[1]])
    for k in range(held_ref.shape[1] // width):
        fill_held(held_ref, k * width, t_ref[first + k, :dim, :])
    LogSums(stream_ref, held_ref, extra_ref, out_ref, shift_ref, column_blocks).run()


def first_column_kernel(*refs):
    ins, (t_ref, bias_ref, out_ref, stream_ref), scratch = refs[:-7], refs[-7:-3], refs[-3:]
    fill_column_stream(*ins, stream_ref)
    columns(0, t_ref, bias_ref, out_ref, stream_ref, *scratch)


def next_column_kernel(first, stream_ref, t_ref, bias_ref, out_ref, *scratch):
    columns(first, t_ref, bias_ref, out_ref, stream_ref, *scratch)


whole = pl.BlockSpec(memory_space=pltpu.VMEM)


def call(kernel, name, operands, outs, scratch):
    return pl.pallas_call(
        kernel,
        in_specs=[whole] * len(operands),
        out_specs=[whole] * len(outs),
        out_shape=[jax.ShapeDtypeStruct(*o) for o in outs],
        scratch_shapes=[pltpu.VMEM(*s) for s in scratch],
        compiler_params=pltpu.CompilerParams(vmem_limit_bytes=40 * 2**20),
        name=name,
    )(*operands)


def stream_of(points):
    return ((points, 128), jnp.bfloat16)


def arrays_of(n):
    row = ((1, n), jnp.float32)
    return row, ((2 * dim, n), jnp.bfloat16), ((16, n), jnp.bfloat16)


def points_of(targets):
    return targets.shape[0] * targets.shape[2]


def first_row_sums(targets, sources):
    row, held, extra = arrays_of(points_of(sources))
    outs = (row, held, row, arrays_of(points_of(targets))[0])
    scratch = (stream_of(points_of(targets)), extra)
    return call(first_row_kernel, "first_row_sums", (targets, sources), outs, scratch)


def next_row_sums(targets, prior, held, shift):
    row, _, extra = arrays_of(held.shape[1])
    outs = (row, arrays_of(points_of(targets))[0])
    scratch = (stream_of(points_of(targets)), extra, row)
    return call(next_row_kernel, "next_row_sums", (targets, held, shift, prior), outs, scratch)


def first_column_sums(targets, biases, sources, *more):
    row, held, extra = arrays_of(points_of(targets))
    operands = (sources, *more, targets, biases)
    outs = (row, stream_of(points_of(sources)))
    return call(first_column_kernel, "first_column_sums", operands, outs, (held, extra, row))


def next_column_sums(stream, targets, biases, first, count):
    row, held, extra = arrays_of(count * targets.shape[2])
    kernel = functools.partial(next_column_kernel, first)
    operands = (stream, targets, biases)
    return call(kernel, "next_column_sums", operands, (row,), (held, extra, row))[0]


def exchange(v, axes, flip):
    size = lax.axis_size(axes)
    return lax.ppermute(v, axes, [(i, i ^ flip) for i in range(size)])


def in_order(bit, v, other):
    first = bit == 0
    return jnp.concatenate([jnp.where(first, v, other), jnp.where(first, other, v)], axis=0)


def doubled(v, axes, flip, bit):
    return in_order(bit, v, exchange(v, axes, flip))


def all_along_z(v, z, axis):
    near, wrap, far = (exchange(v, "z", flip) for flip in (1, 3, 2))
    even, low = z % 2 == 0, z < 2
    own = jnp.concatenate([jnp.where(even, v, near), jnp.where(even, near, v)], axis=axis)
    other = jnp.concatenate([jnp.where(even, far, wrap), jnp.where(even, wrap, far)], axis=axis)
    return jnp.concatenate([jnp.where(low, own, other), jnp.where(low, other, own)], axis=axis)


def norms(points):
    wide = points.astype(jnp.float32)
    return jnp.sum(wide * wide, axis=0)


def per_device(source, target, source_logw, target_logw, start_potential):
    z, y, xh, xl, core = (lax.axis_index(name) for name in names)
    width, span = source.shape[1], target.shape[1]

    sources = source[None]
    targets = jnp.concatenate([target, start_potential], axis=0)[None]
    other = exchange(sources, "core", 1)
    sources = jnp.zeros((2, dim, width), sources.dtype)
    sources = lax.dynamic_update_slice(sources, source[None], (core, 0, 0))
    sources = lax.dynamic_update_slice(sources, other, (1 - core, 0, 0))
    sources = doubled(sources, x, 1, xl)
    direct = [exchange(targets, axes, flip) for axes, flip in ((x, 3), ("y", 3), (("y", *x), 15))]
    targets = jnp.concatenate([targets, *direct], axis=0)
    sources = all_along_z(sources, z, 0)
    others = exchange(targets, "y", 1)

    lse, held, shift, biases = first_row_sums(targets, sources)
    lse, other_biases = next_row_sums(others, lse, held, shift)
    column_base = smoothing * target_logw
    lse, column_base = lax.optimization_barrier((lse, column_base))
    lse = log_add(lse, exchange(lse, "core", 1))
    count = lse.shape[1]
    logw = source_logw[None]
    received = [exchange(jnp.concatenate([lse, logw], axis=1), "z", flip) for flip in (1, 3, 2)]
    parts = [v[:, :count] for v in received]
    lse = log_add(log_add(lse, parts[0]), log_add(parts[1], parts[2]))
    near, wrap, far = (v[:, count:] for v in received)
    even, low = z % 2 == 0, z < 2
    own = jnp.concatenate([jnp.where(even, logw, near), jnp.where(even, near, logw)], axis=1)
    other = jnp.concatenate([jnp.where(even, far, wrap), jnp.where(even, wrap, far)], axis=1)
    logw = jnp.where(
        low, jnp.concatenate([own, other], axis=1), jnp.concatenate([other, own], axis=1)
    )
    received = exchange(lse, x, 1)
    partial, stream = first_column_sums(others, other_biases, sources, lse, received, logw)
    sent = exchange(partial, "y", 1)
    half = 2 * span
    partial = next_column_sums(stream, targets, biases, 2, 2)
    partial = log_add(partial, sent[:, half:])
    more = exchange(partial, "y", 3)
    partial = next_column_sums(stream, targets, biases, 1, 1)
    partial = log_add(log_add(partial, sent[:, span:half]), more[:, span:])

    at = z
    lse = log_add(lse, received)
    mine = lax.dynamic_index_in_dim(lse.reshape(4, 4 * width), at, 0, False)
    picked = lax.dynamic_index_in_dim(sources.reshape(4, 4, dim, width), at, 0, False)
    row_sq = jnp.sum(jnp.square(picked.astype(jnp.float32)), axis=1).reshape(4 * width)
    row_lse = mine / log2e - row_sq / smoothing
    row_potential = smoothing * source_logw - smoothing * row_lse
    partial, row_potential = lax.optimization_barrier((partial, row_potential))
    last = exchange(partial, x, 3)
    partial = next_column_sums(stream, targets, biases, 0, 1)
    partial = log_add(log_add(partial, sent[:, :span]), more[:, :span])
    partial = log_add(partial, last)[0]

    col_lse = partial / log2e - norms(target) / smoothing
    col_potential = column_base - smoothing * col_lse
    return (row_potential, col_potential)


def solution(mesh):
    devices = Mesh(mesh.devices.reshape(shape), names)
    rows = ("z", "y", "xh")
    columns_over = ("xl", "core", "z", "y", "xh")
    in_specs = (P(None, names), P(None, columns_over), P(rows), P(columns_over), P(None, columns_over))
    out_specs = (P(rows), P(columns_over))
    return jax.shard_map(
        per_device, mesh=devices, in_specs=in_specs, out_specs=out_specs, check_vma=False
    )
```

profile of v0, /device:TPU:8, one launch (start us, length us, event | category | flops | bytes accessed | tf_op | source)
XLA Modules:
  0.0 141.7 jit_solution(5319222609618590250)
XLA Ops:
  0.6 0.1 collective-permute-start
  0.8 0.7 copy-done.2
  1.5 0.6 collective-permute-done
  2.1 1.5 %collective-permute-start.1 = (bf16[2,64,256]{2,1,0:T(8,128)(2,1)S(1)}, bf16[2,64,256]{2,1,0:T(8,128)(2,1)S(1)}, u32[]{:S(2)}, u32[]{:S(2)}) collective-permute-start(bf16[2,64,256]{2,1,0:T(8,128)(2,1)S(1)} %constant_dynamic-update-slice_fusion), channel_id=1, source_target_pairs={{0,2},{2,0},{4,6},{6,4},{1,3},{3,1},{5,7},{7,5},{8,10},{10,8},{12,... | collective-permute-start | bytes 196616 | tf_op jit(solution)/shard_map/ppermute | solution.py:264
  3.6 2.2 %collective-permute-start.5 = (bf16[1,65,768]{2,1,0:T(8,128)(2,1)S(1)}, bf16[1,65,768]{2,1,0:T(8,128)(2,1)S(1)}, u32[]{:S(2)}, u32[]{:S(2)}) collective-permute-start(bf16[1,65,768]{2,1,0:T(8,128)(2,1)S(1)} %maximum_bitcast_fusion), channel_id=1, source_target_pairs={{0,6},{2,4},{4,2},{6,0},{1,7},{3,5},{5,3},{7,1},{8,14},{10,12},{12... | collective-permute-start | bytes 299528 | tf_op jit(solution)/shard_map/ppermute | solution.py:264
  5.8 1.6 %collective-permute-start.6 = (bf16[1,65,768]{2,1,0:T(8,128)(2,1)S(1)}, bf16[1,65,768]{2,1,0:T(8,128)(2,1)S(1)}, u32[]{:S(2)}, u32[]{:S(2)}) collective-permute-start(bf16[1,65,768]{2,1,0:T(8,128)(2,1)S(1)} %maximum_bitcast_fusion), channel_id=1, source_target_pairs={{0,24},{8,16},{16,8},{24,0},{1,25},{9,17},{17,9},{25,1},{2,26},{10... | collective-permute-start | bytes 299528 | tf_op jit(solution)/shard_map/ppermute | solution.py:264
  7.4 1.0 collective-permute-start.7
  8.4 0.0 collective-permute-done.1
  8.4 0.0 copy-start.3
  8.5 4.0 %collective-permute-start.3 = (bf16[4,64,256]{2,1,0:T(8,128)(2,1)S(1)}, bf16[4,64,256]{2,1,0:T(8,128)(2,1)S(1)}, u32[]{:S(2)}, u32[]{:S(2)}) collective-permute-start(bf16[4,64,256]{2,1,0:T(8,128)(2,1)S(1)} %pad_maximum_fusion.4), channel_id=1, source_target_pairs={{0,64},{32,96},{64,0},{96,32},{1,65},{33,97},{65,1},{97,33},{2,66}... | collective-permute-start | bytes 393224 | tf_op jit(solution)/shard_map/ppermute | solution.py:264
  12.4 0.7 collective-permute-start.4
  13.2 0.4 collective-permute-start.2
  13.6 0.0 collective-permute-done.6
  13.6 0.7 collective-permute-done.7
  14.3 0.1 pad_maximum_fusion.1.t_ref
  14.3 3.2 %collective-permute-start.8 = (bf16[4,65,768]{2,1,0:T(8,128)(2,1)S(1)}, bf16[4,65,768]{2,1,0:T(8,128)(2,1)S(1)}, u32[]{:S(2)}, u32[]{:S(2)}) collective-permute-start(bf16[4,65,768]{2,1,0:T(8,128)(2,1)S(1)} %pad_maximum_fusion.1.t_ref), channel_id=1, source_target_pairs={{0,8},{8,0},{16,24},{24,16},{1,9},{9,1},{17,25},{25,17},{2,10},{10... | collective-permute-start | bytes 1198088 | tf_op jit(solution)/shard_map/ppermute | solution.py:264
  17.5 0.0 collective-permute-done.3
  17.5 1.1 collective-permute-done.4
  18.6 0.1 collective-permute-done.2
  18.8 0.1 broadcast_select_fusion.1
  18.9 29.3 %first_row_sums.1 = (f32[1,4096]{1,0:T(1,128)S(1)}, bf16[128,4096]{1,0:T(8,128)(2,1)S(1)}, f32[1,4096]{1,0:T(1,128)S(1)}, f32[1,3072]{1,0:T(1,128)S(1)}) custom-call(bf16[4,65,768]{2,1,0:T(8,128)(2,1)S(1)} %pad_maximum_fusion.1.t_ref, bf16[16,64,256]{2,1,0:T(8,128)(2,1)S(1)} %pad_maximum_fusion.s_ref.refs_0_), custom_call_target="tpu_custom_call" | custom-call | tf_op jit(solution)/shard_map/first_row_sums/pallas_call | solution.py:210
  48.2 0.0 collective-permute-done.8.t_ref.refs_4_
  48.2 7.3 %next_row_sums.1 = (f32[1,4096]{1,0:T(1,128)S(1)}, f32[1,3072]{1,0:T(1,128)S(1)}) custom-call(bf16[4,65,768]{2,1,0:T(8,128)(2,1)S(1)} %collective-permute-done.8.t_ref.refs_4_, bf16[128,4096]{1,0:T(8,128)(2,1)S(1)} %get-tuple-element.14.held_ref, f32[1,4096]{1,0:T(1,128)S(1)} %get-tuple-element.15.old_ref, f32[1,4096]{1,0:T(1,128)S(1)} %get-tuple-element.16.prior_ref), custom_call_target="tpu_custom_call" | custom-call | tf_op jit(solution)/shard_map/next_row_sums/pallas_call | solution.py:210
  55.5 0.3 collective-permute-start.9
  55.8 0.0 copy-start.1
  55.9 1.1 collective-permute-done.9
  57.0 0.1 multiply_add_fusion.1
  57.1 2.9 %collective-permute-start.11 = (f32[1,5120]{1,0:T(1,128)S(1)}, f32[1,5120]{1,0:T(1,128)S(1)}, u32[]{:S(2)}, u32[]{:S(2)}) collective-permute-start(f32[1,5120]{1,0:T(1,128)S(1)} %pad_maximum_fusion.5), channel_id=1, source_target_pairs={{0,96},{32,64},{64,32},{96,0},{1,97},{33,65},{65,33},{97,1},{2,98}... | collective-permute-start | bytes 61448 | tf_op jit(solution)/shard_map/ppermute | solution.py:264
  60.0 0.2 collective-permute-start.12
  60.2 1.0 collective-permute-start.10
  61.3 0.9 collective-permute-done.11
  62.1 3.1 %collective-permute-done.12 = f32[1,5120]{1,0:T(1,128)S(1)} collective-permute-done((f32[1,5120]{1,0:T(1,128)S(1)}, f32[1,5120]{1,0:T(1,128)S(1)}, u32[]{:S(2)}, u32[]{:S(2)}) %collective-permute-start.12) | collective-permute-done | bytes 20512 | tf_op jit(solution)/shard_map/ppermute | solution.py:264
  65.3 0.0 collective-permute-done.10
  65.3 0.2 multiply_add_fusion.refs_1_
  65.5 0.1 collective-permute-start.13
  65.6 3.7 %collective-permute-done.13.refs_2_ = f32[1,4096]{1,0:T(1,128)S(1)} collective-permute-done((f32[1,4096]{1,0:T(1,128)S(1)}, f32[1,4096]{1,0:T(1,128)S(1)}, u32[]{:S(2)}, u32[]{:S(2)}) %collective-permute-start.13) | collective-permute-done | bytes 16416 | tf_op jit(solution)/shard_map/ppermute | solution.py:264
  69.3 0.1 add_reduce_fusion
  69.4 31.9 %first_column_sums.1 = (f32[1,3072]{1,0:T(1,128)S(1)}, bf16[4096,128]{1,0:T(8,128)(2,1)S(1)}) custom-call(bf16[16,64,256]{2,1,0:T(8,128)(2,1)S(1)} %pad_maximum_fusion.s_ref.refs_0_, f32[1,4096]{1,0:T(1,128)S(1)} %multiply_add_fusion.refs_1_, f32[1,4096]{1,0:T(1,128)S(1)} %collective-permute-done.13.refs_2_, f32[1,4096]{1,0:T(1,128)S(1)} %broadcast_select_fusion.8.refs_3_, ...), custom_call_target="tpu_custom_call" | custom-call | tf_op jit(solution)/shard_map/first_column_sums/pallas_call | solution.py:210
  101.3 1.6 %collective-permute-start.14 = (f32[1,3072]{1,0:T(1,128)S(1)}, f32[1,3072]{1,0:T(1,128)S(1)}, u32[]{:S(2)}, u32[]{:S(2)}) collective-permute-start(f32[1,3072]{1,0:T(1,128)S(1)} %get-tuple-element.22), channel_id=1, source_target_pairs={{0,8},{8,0},{16,24},{24,16},{1,9},{9,1},{17,25},{25,17},{2,10},{10... | collective-permute-start | bytes 36872 | tf_op jit(solution)/shard_map/ppermute | solution.py:264
  102.9 16.2 %next_column_sums.4 = f32[1,1536]{1,0:T(1,128)S(1)} custom-call(bf16[4096,128]{1,0:T(8,128)(2,1)S(1)} %get-tuple-element.20.stream_ref, bf16[4,65,768]{2,1,0:T(8,128)(2,1)S(1)} %pad_maximum_fusion.1.t_ref, f32[1,3072]{1,0:T(1,128)S(1)} %get-tuple-element.21.bias_ref), custom_call_target="tpu_custom_call" | custom-call | tf_op jit(solution)/shard_map/next_column_sums/pallas_call | solution.py:210
  119.2 2.4 %collective-permute-start.15 = (f32[1,1536]{1,0:T(1,128)S(1)}, f32[1,1536]{1,0:T(1,128)S(1)}, u32[]{:S(2)}, u32[]{:S(2)}) collective-permute-start(f32[1,1536]{1,0:T(1,128)S(1)} %multiply_add_fusion.2), channel_id=1, source_target_pairs={{0,24},{8,16},{16,8},{24,0},{1,25},{9,17},{17,9},{25,1},{2,26},{10... | collective-permute-start | bytes 18440 | tf_op jit(solution)/shard_map/ppermute | solution.py:264
  121.6 0.6 multiply_subtract_fusion.1
  122.2 8.2 %next_column_sums.3 = f32[1,768]{1,0:T(1,128)S(1)} custom-call(bf16[4096,128]{1,0:T(8,128)(2,1)S(1)} %get-tuple-element.20.stream_ref, bf16[4,65,768]{2,1,0:T(8,128)(2,1)S(1)} %pad_maximum_fusion.1.t_ref, f32[1,3072]{1,0:T(1,128)S(1)} %get-tuple-element.21.bias_ref), custom_call_target="tpu_custom_call" | custom-call | tf_op jit(solution)/shard_map/next_column_sums/pallas_call | solution.py:210
  130.5 2.2 %collective-permute-start.16 = (f32[1,768]{1,0:T(1,128)S(1)}, f32[1,768]{1,0:T(1,128)S(1)}, u32[]{:S(2)}, u32[]{:S(2)}) collective-permute-start(f32[1,768]{1,0:T(1,128)S(1)} %multiply_add_fusion.3), channel_id=1, source_target_pairs={{0,6},{2,4},{4,2},{6,0},{1,7},{3,5},{5,3},{7,1},{8,14},{10,12},{12... | collective-permute-start | bytes 9224 | tf_op jit(solution)/shard_map/ppermute | solution.py:264
  132.7 8.2 %next_column_sums.5 = f32[1,768]{1,0:T(1,128)S(1)} custom-call(bf16[4096,128]{1,0:T(8,128)(2,1)S(1)} %get-tuple-element.20.stream_ref, bf16[4,65,768]{2,1,0:T(8,128)(2,1)S(1)} %pad_maximum_fusion.1.t_ref, f32[1,3072]{1,0:T(1,128)S(1)} %get-tuple-element.21.bias_ref), custom_call_target="tpu_custom_call" | custom-call | tf_op jit(solution)/shard_map/next_column_sums/pallas_call | solution.py:210
  141.0 0.0 collective-permute-done.16
  141.0 0.1 multiply_reduce_fusion.2
  141.1 0.6 multiply_subtract_fusion
  (32 shorter events, 0.4 us)
Async XLA Ops:
  0.6 1.5 %collective-permute-start = (bf16[1,64,256]{2,1,0:T(8,128)(2,1)}, bf16[1,64,256]{2,1,0:T(8,128)(2,1)S(1)}, u32[]{:S(2)}, u32[]{:S(2)}) collective-permute-start(bf16[1,64,256]{2,1,0:T(8,128)(2,1)} %bitcast.13), channel_id=1, source_target_pairs={{0,1},{1,0},{2,3},{3,2},{4,5},{5,4},{6,7},{7,6},{8,9},{9,8},{10,11... | collective-permute-start | bytes 98312 | tf_op jit(solution)/shard_map/ppermute | solution.py:264
  0.7 0.8 copy-start.2
  0.7 2.9 %copy-start = (bf16[64,768]{1,0:T(8,128)(2,1)S(1)}, bf16[64,768]{1,0:T(8,128)(2,1)}, u32[]{:S(2)}) copy-start(bf16[64,768]{1,0:T(8,128)(2,1)} %param.6) | copy-start | bytes 294916
  1.5 2.1 %copy-start.4 = (bf16[1,768]{1,0:T(2,128)(2,1)S(1)}, bf16[1,768]{1,0:T(2,128)(2,1)}, u32[]{:S(2)}) copy-start(bf16[1,768]{1,0:T(2,128)(2,1)} %param.9) | copy-start | bytes 4612
  2.1 6.3 %collective-permute-start.1 = (bf16[2,64,256]{2,1,0:T(8,128)(2,1)S(1)}, bf16[2,64,256]{2,1,0:T(8,128)(2,1)S(1)}, u32[]{:S(2)}, u32[]{:S(2)}) collective-permute-start(bf16[2,64,256]{2,1,0:T(8,128)(2,1)S(1)} %constant_dynamic-update-slice_fusion), channel_id=1, source_target_pairs={{0,2},{2,0},{4,6},{6,4},{1,3},{3,1},{5,7},{7,5},{8,10},{10,8},{12,... | collective-permute-start | bytes 196616 | tf_op jit(solution)/shard_map/ppermute | solution.py:264
  3.6 9.5 %collective-permute-start.5 = (bf16[1,65,768]{2,1,0:T(8,128)(2,1)S(1)}, bf16[1,65,768]{2,1,0:T(8,128)(2,1)S(1)}, u32[]{:S(2)}, u32[]{:S(2)}) collective-permute-start(bf16[1,65,768]{2,1,0:T(8,128)(2,1)S(1)} %maximum_bitcast_fusion), channel_id=1, source_target_pairs={{0,6},{2,4},{4,2},{6,0},{1,7},{3,5},{5,3},{7,1},{8,14},{10,12},{12... | collective-permute-start | bytes 299528 | tf_op jit(solution)/shard_map/ppermute | solution.py:264
  5.8 7.8 %collective-permute-start.6 = (bf16[1,65,768]{2,1,0:T(8,128)(2,1)S(1)}, bf16[1,65,768]{2,1,0:T(8,128)(2,1)S(1)}, u32[]{:S(2)}, u32[]{:S(2)}) collective-permute-start(bf16[1,65,768]{2,1,0:T(8,128)(2,1)S(1)} %maximum_bitcast_fusion), channel_id=1, source_target_pairs={{0,24},{8,16},{16,8},{24,0},{1,25},{9,17},{17,9},{25,1},{2,26},{10... | collective-permute-start | bytes 299528 | tf_op jit(solution)/shard_map/ppermute | solution.py:264
  7.4 6.9 %collective-permute-start.7 = (bf16[1,65,768]{2,1,0:T(8,128)(2,1)S(1)}, bf16[1,65,768]{2,1,0:T(8,128)(2,1)S(1)}, u32[]{:S(2)}, u32[]{:S(2)}) collective-permute-start(bf16[1,65,768]{2,1,0:T(8,128)(2,1)S(1)} %maximum_bitcast_fusion), channel_id=1, source_target_pairs={{0,30},{2,28},{4,26},{6,24},{8,22},{10,20},{12,18},{14,16},{16,14}... | collective-permute-start | bytes 299528 | tf_op jit(solution)/shard_map/ppermute | solution.py:264
  8.4 4.7 %copy-start.3 = (f32[768]{0:T(1024)S(1)}, f32[768]{0:T(1024)}, u32[]{:S(2)}) copy-start(f32[768]{0:T(1024)} %param.8) | copy-start | bytes 9220
  8.5 9.0 %collective-permute-start.3 = (bf16[4,64,256]{2,1,0:T(8,128)(2,1)S(1)}, bf16[4,64,256]{2,1,0:T(8,128)(2,1)S(1)}, u32[]{:S(2)}, u32[]{:S(2)}) collective-permute-start(bf16[4,64,256]{2,1,0:T(8,128)(2,1)S(1)} %pad_maximum_fusion.4), channel_id=1, source_target_pairs={{0,64},{32,96},{64,0},{96,32},{1,65},{33,97},{65,1},{97,33},{2,66}... | collective-permute-start | bytes 393224 | tf_op jit(solution)/shard_map/ppermute | solution.py:264
  12.4 6.2 %collective-permute-start.4 = (bf16[4,64,256]{2,1,0:T(8,128)(2,1)S(1)}, bf16[4,64,256]{2,1,0:T(8,128)(2,1)S(1)}, u32[]{:S(2)}, u32[]{:S(2)}) collective-permute-start(bf16[4,64,256]{2,1,0:T(8,128)(2,1)S(1)} %pad_maximum_fusion.4), channel_id=1, source_target_pairs={{0,96},{32,64},{64,32},{96,0},{1,97},{33,65},{65,33},{97,1},{2,98}... | collective-permute-start | bytes 393224 | tf_op jit(solution)/shard_map/ppermute | solution.py:264
  13.2 5.6 %collective-permute-start.2 = (bf16[4,64,256]{2,1,0:T(8,128)(2,1)S(1)}, bf16[4,64,256]{2,1,0:T(8,128)(2,1)S(1)}, u32[]{:S(2)}, u32[]{:S(2)}) collective-permute-start(bf16[4,64,256]{2,1,0:T(8,128)(2,1)S(1)} %pad_maximum_fusion.4), channel_id=1, source_target_pairs={{0,32},{32,0},{64,96},{96,64},{1,33},{33,1},{65,97},{97,65},{2,34}... | collective-permute-start | bytes 393224 | tf_op jit(solution)/shard_map/ppermute | solution.py:264
  14.3 33.8 %collective-permute-start.8 = (bf16[4,65,768]{2,1,0:T(8,128)(2,1)S(1)}, bf16[4,65,768]{2,1,0:T(8,128)(2,1)S(1)}, u32[]{:S(2)}, u32[]{:S(2)}) collective-permute-start(bf16[4,65,768]{2,1,0:T(8,128)(2,1)S(1)} %pad_maximum_fusion.1.t_ref), channel_id=1, source_target_pairs={{0,8},{8,0},{16,24},{24,16},{1,9},{9,1},{17,25},{25,17},{2,10},{10... | collective-permute-start | bytes 1198088 | tf_op jit(solution)/shard_map/ppermute | solution.py:264
  55.5 1.4 %collective-permute-start.9 = (f32[1,4096]{1,0:T(1,128)S(1)}, f32[1,4096]{1,0:T(1,128)S(1)}, u32[]{:S(2)}, u32[]{:S(2)}) collective-permute-start(f32[1,4096]{1,0:T(1,128)S(1)} %get-tuple-element.18), channel_id=1, source_target_pairs={{0,1},{1,0},{2,3},{3,2},{4,5},{5,4},{6,7},{7,6},{8,9},{9,8},{10,11... | collective-permute-start | bytes 49160 | tf_op jit(solution)/shard_map/ppermute | solution.py:264
  55.8 1.2 copy-start.1
  57.1 5.1 %collective-permute-start.11 = (f32[1,5120]{1,0:T(1,128)S(1)}, f32[1,5120]{1,0:T(1,128)S(1)}, u32[]{:S(2)}, u32[]{:S(2)}) collective-permute-start(f32[1,5120]{1,0:T(1,128)S(1)} %pad_maximum_fusion.5), channel_id=1, source_target_pairs={{0,96},{32,64},{64,32},{96,0},{1,97},{33,65},{65,33},{97,1},{2,98}... | collective-permute-start | bytes 61448 | tf_op jit(solution)/shard_map/ppermute | solution.py:264
  60.0 5.3 %collective-permute-start.12 = (f32[1,5120]{1,0:T(1,128)S(1)}, f32[1,5120]{1,0:T(1,128)S(1)}, u32[]{:S(2)}, u32[]{:S(2)}) collective-permute-start(f32[1,5120]{1,0:T(1,128)S(1)} %pad_maximum_fusion.5), channel_id=1, source_target_pairs={{0,64},{32,96},{64,0},{96,32},{1,65},{33,97},{65,1},{97,33},{2,66}... | collective-permute-start | bytes 61448 | tf_op jit(solution)/shard_map/ppermute | solution.py:264
  60.2 5.1 %collective-permute-start.10 = (f32[1,5120]{1,0:T(1,128)S(1)}, f32[1,5120]{1,0:T(1,128)S(1)}, u32[]{:S(2)}, u32[]{:S(2)}) collective-permute-start(f32[1,5120]{1,0:T(1,128)S(1)} %pad_maximum_fusion.5), channel_id=1, source_target_pairs={{0,32},{32,0},{64,96},{96,64},{1,33},{33,1},{65,97},{97,65},{2,34}... | collective-permute-start | bytes 61448 | tf_op jit(solution)/shard_map/ppermute | solution.py:264
  65.5 3.8 %collective-permute-start.13 = (f32[1,4096]{1,0:T(1,128)S(1)}, f32[1,4096]{1,0:T(1,128)S(1)}, u32[]{:S(2)}, u32[]{:S(2)}) collective-permute-start(f32[1,4096]{1,0:T(1,128)S(1)} %multiply_add_fusion.refs_1_), channel_id=1, source_target_pairs={{0,2},{2,0},{4,6},{6,4},{1,3},{3,1},{5,7},{7,5},{8,10},{10,8},{12,... | collective-permute-start | bytes 49160 | tf_op jit(solution)/shard_map/ppermute | solution.py:264
  101.3 17.8 %collective-permute-start.14 = (f32[1,3072]{1,0:T(1,128)S(1)}, f32[1,3072]{1,0:T(1,128)S(1)}, u32[]{:S(2)}, u32[]{:S(2)}) collective-permute-start(f32[1,3072]{1,0:T(1,128)S(1)} %get-tuple-element.22), channel_id=1, source_target_pairs={{0,8},{8,0},{16,24},{24,16},{1,9},{9,1},{17,25},{25,17},{2,10},{10... | collective-permute-start | bytes 36872 | tf_op jit(solution)/shard_map/ppermute | solution.py:264
  119.2 11.3 %collective-permute-start.15 = (f32[1,1536]{1,0:T(1,128)S(1)}, f32[1,1536]{1,0:T(1,128)S(1)}, u32[]{:S(2)}, u32[]{:S(2)}) collective-permute-start(f32[1,1536]{1,0:T(1,128)S(1)} %multiply_add_fusion.2), channel_id=1, source_target_pairs={{0,24},{8,16},{16,8},{24,0},{1,25},{9,17},{17,9},{25,1},{2,26},{10... | collective-permute-start | bytes 18440 | tf_op jit(solution)/shard_map/ppermute | solution.py:264
  130.5 10.5 %collective-permute-start.16 = (f32[1,768]{1,0:T(1,128)S(1)}, f32[1,768]{1,0:T(1,128)S(1)}, u32[]{:S(2)}, u32[]{:S(2)}) collective-permute-start(f32[1,768]{1,0:T(1,128)S(1)} %multiply_add_fusion.3), channel_id=1, source_target_pairs={{0,6},{2,4},{4,2},{6,0},{1,7},{3,5},{5,3},{7,1},{8,14},{10,12},{12... | collective-permute-start | bytes 9224 | tf_op jit(solution)/shard_map/ppermute | solution.py:264
where the time goes:
time: 142 us
  Pallas kernels  101 us (71%)
  starting transfers between devices  25.3 us (18%)
  waiting for transfers between devices  11.3 us (8%)
  other arithmetic  2.07 us (1%)
    pallas_call x6, Pallas kernels, call(): pl.pallas_call(kernel, in_specs=[whole] * len(operands), out_specs=[whole...  101 us
    ppermute x17, starting transfers between devices, exchange(): return lax.ppermute(v, axes, [(i, i ^ flip) for i in range(size)])  25.3 us
    ppermute x17, waiting for transfers between devices, exchange(): return lax.ppermute(v, axes, [(i, i ^ flip) for i in range(size)])  11.3 us
  transfers between devices with their start and end apart: 17, of which 8 were waited for; matrix products, arithmetic and copies ran while one was open for 1% of the time, Pallas kernels for 44%

commit v1 on v0

--- a/solution.py
+++ b/solution.py
@@ -173,13 +173,13 @@
     LogSums(stream_ref, held_ref, extra_ref, out_ref, shift_ref, row_blocks).run(prior_ref[...])
 
 
-def fill_column_stream(s_ref, lse_ref, received_ref, logw_ref, stream_ref):
+def fill_column_stream(s_ref, lse_ref, near_ref, far_ref, logw_ref, stream_ref):
     pieces, _, width = s_ref.shape
     per = pieces // len(along_z)
     for k in range(pieces):
         at = (along_z[k // per] * per + k % per) * width
         cols = slice(k * width, (k + 1) * width)
-        lse = log_add(lse_ref[:, cols], received_ref[:, cols])
+        lse = log_add(lse_ref[:, cols], log_add(near_ref[:, cols], far_ref[:, cols]))
         bias = log2e * logw_ref[:, at : at + width] - lse
         stream_ref[cols, :] = streamed_features(s_ref[k], bias)
 
@@ -274,7 +274,7 @@
 
 
 def all_along_z(v, z, axis):
-    near, wrap, far = (exchange(v, "z", flip) for flip in (1, 3, 2))
+    far, wrap, near = (exchange(v, "z", flip) for flip in (2, 3, 1))
     even, low = z % 2 == 0, z < 2
     own = jnp.concatenate([jnp.where(even, v, near), jnp.where(even, near, v)], axis=axis)
     other = jnp.concatenate([jnp.where(even, far, wrap), jnp.where(even, wrap, far)], axis=axis)
@@ -306,21 +306,22 @@
     lse, other_biases = next_row_sums(others, lse, held, shift)
     column_base = smoothing * target_logw
     lse, column_base = lax.optimization_barrier((lse, column_base))
-    lse = log_add(lse, exchange(lse, "core", 1))
     count = lse.shape[1]
     logw = source_logw[None]
-    received = [exchange(jnp.concatenate([lse, logw], axis=1), "z", flip) for flip in (1, 3, 2)]
+    received = [exchange(jnp.concatenate([lse, logw], axis=1), "z", flip) for flip in (2, 3, 1)]
     parts = [v[:, :count] for v in received]
     lse = log_add(log_add(lse, parts[0]), log_add(parts[1], parts[2]))
-    near, wrap, far = (v[:, count:] for v in received)
+    far, wrap, near = (v[:, count:] for v in received)
     even, low = z % 2 == 0, z < 2
     own = jnp.concatenate([jnp.where(even, logw, near), jnp.where(even, near, logw)], axis=1)
     other = jnp.concatenate([jnp.where(even, far, wrap), jnp.where(even, wrap, far)], axis=1)
     logw = jnp.where(
         low, jnp.concatenate([own, other], axis=1), jnp.concatenate([other, own], axis=1)
     )
-    received = exchange(lse, x, 1)
-    partial, stream = first_column_sums(others, other_biases, sources, lse, received, logw)
+    beside = exchange(lse, x, 1)
+    across = exchange(lse, (*x, "core"), 3)
+    lse = log_add(lse, exchange(lse, "core", 1))
+    partial, stream = first_column_sums(others, other_biases, sources, lse, beside, across, logw)
     sent = exchange(partial, "y", 1)
     half = 2 * span
     partial = next_column_sums(stream, targets, biases, 2, 2)
@@ -330,7 +331,7 @@
     partial = log_add(log_add(partial, sent[:, span:half]), more[:, span:])
 
     at = z
-    lse = log_add(lse, received)
+    lse = log_add(lse, log_add(beside, across))
     mine = lax.dynamic_index_in_dim(lse.reshape(4, 4 * width), at, 0, False)
     picked = lax.dynamic_index_in_dim(sources.reshape(4, 4, dim, width), at, 0, False)
     row_sq = jnp.sum(jnp.square(picked.astype(jnp.float32)), axis=1).reshape(4 * width)

time: 142 us -> 142 us (level)
    ppermute x17 -> x18, waiting for transfers between devices: 11.3 us -> 9.99 us  [exchange(): return lax.ppermute(v, axes, [(i, i ^ flip) for i in range(size)])]
    ppermute x17 -> x18, starting transfers between devices: 25.3 us -> 26.2 us  [exchange(): return lax.ppermute(v, axes, [(i, i ^ flip) for i in range(size)])]
  transfers between devices with their start and end apart: 17 -> 18, of which waited for: 8 -> 6; matrix products, arithmetic and copies ran while one was open for 1% -> 1% of each run, Pallas kernels for 44% -> 44%
where the time goes in v1:
time: 142 us; the launch traced here: 141 us
  Pallas kernels  101 us (71%)
  starting transfers between devices  26.2 us (18%)
  waiting for transfers between devices  9.99 us (7%)
  other arithmetic  2.1 us (1%)
    pallas_call x6, Pallas kernels, call(): pl.pallas_call(kernel, in_specs=[whole] * len(operands), out_specs=[whole...  101 us
    ppermute x18, starting transfers between devices, exchange(): return lax.ppermute(v, axes, [(i, i ^ flip) for i in range(size)])  26.2 us
    ppermute x18, waiting for transfers between devices, exchange(): return lax.ppermute(v, axes, [(i, i ^ flip) for i in range(size)])  9.99 us
  transfers between devices with their start and end apart: 18, of which 6 were waited for; matrix products, arithmetic and copies ran while one was open for 1% of the time, Pallas kernels for 44%

profile of v1, /device:TPU:8, one launch (start us, length us, event | category | flops | bytes accessed | tf_op | source)
XLA Modules:
  0.0 141.2 jit_solution(9417433202176604733)
XLA Ops:
  0.6 0.1 collective-permute-start
  0.8 0.7 copy-done.2
  1.5 0.6 collective-permute-done
  2.1 1.5 %collective-permute-start.1 = (bf16[2,64,256]{2,1,0:T(8,128)(2,1)S(1)}, bf16[2,64,256]{2,1,0:T(8,128)(2,1)S(1)}, u32[]{:S(2)}, u32[]{:S(2)}) collective-permute-start(bf16[2,64,256]{2,1,0:T(8,128)(2,1)S(1)} %constant_dynamic-update-slice_fusion), channel_id=1, source_target_pairs={{0,2},{2,0},{4,6},{6,4},{1,3},{3,1},{5,7},{7,5},{8,10},{10,8},{12,... | collective-permute-start | bytes 196616 | tf_op jit(solution)/shard_map/ppermute | solution.py:264
  3.6 3.2 %collective-permute-start.7 = (bf16[1,65,768]{2,1,0:T(8,128)(2,1)S(1)}, bf16[1,65,768]{2,1,0:T(8,128)(2,1)S(1)}, u32[]{:S(2)}, u32[]{:S(2)}) collective-permute-start(bf16[1,65,768]{2,1,0:T(8,128)(2,1)S(1)} %maximum_bitcast_fusion), channel_id=1, source_target_pairs={{0,30},{2,28},{4,26},{6,24},{8,22},{10,20},{12,18},{14,16},{16,14}... | collective-permute-start | bytes 299528 | tf_op jit(solution)/shard_map/ppermute | solution.py:264
  6.8 0.4 collective-permute-start.6
  7.3 1.1 collective-permute-start.5
  8.4 0.0 collective-permute-done.1
  8.4 0.0 copy-start.3
  8.5 4.1 %collective-permute-start.4 = (bf16[4,64,256]{2,1,0:T(8,128)(2,1)S(1)}, bf16[4,64,256]{2,1,0:T(8,128)(2,1)S(1)}, u32[]{:S(2)}, u32[]{:S(2)}) collective-permute-start(bf16[4,64,256]{2,1,0:T(8,128)(2,1)S(1)} %pad_maximum_fusion.4), channel_id=1, source_target_pairs={{0,96},{32,64},{64,32},{96,0},{1,97},{33,65},{65,33},{97,1},{2,98}... | collective-permute-start | bytes 393224 | tf_op jit(solution)/shard_map/ppermute | solution.py:264
  12.6 0.0 collective-permute-start.3
  12.6 1.0 collective-permute-start.2
  13.6 0.1 pad_maximum_fusion.1.t_ref
  13.7 1.7 %collective-permute-start.8 = (bf16[4,65,768]{2,1,0:T(8,128)(2,1)S(1)}, bf16[4,65,768]{2,1,0:T(8,128)(2,1)S(1)}, u32[]{:S(2)}, u32[]{:S(2)}) collective-permute-start(bf16[4,65,768]{2,1,0:T(8,128)(2,1)S(1)} %pad_maximum_fusion.1.t_ref), channel_id=1, source_target_pairs={{0,8},{8,0},{16,24},{24,16},{1,9},{9,1},{17,25},{25,17},{2,10},{10... | collective-permute-start | bytes 1198088 | tf_op jit(solution)/shard_map/ppermute | solution.py:264
  15.5 2.0 %collective-permute-done.4 = bf16[4,64,256]{2,1,0:T(8,128)(2,1)S(1)} collective-permute-done((bf16[4,64,256]{2,1,0:T(8,128)(2,1)S(1)}, bf16[4,64,256]{2,1,0:T(8,128)(2,1)S(1)}, u32[]{:S(2)}, u32[]{:S(2)}) %collective-permute-start.4) | collective-permute-done | bytes 131104 | tf_op jit(solution)/shard_map/ppermute | solution.py:264
  17.4 2.3 %collective-permute-done.3 = bf16[4,64,256]{2,1,0:T(8,128)(2,1)S(1)} collective-permute-done((bf16[4,64,256]{2,1,0:T(8,128)(2,1)S(1)}, bf16[4,64,256]{2,1,0:T(8,128)(2,1)S(1)}, u32[]{:S(2)}, u32[]{:S(2)}) %collective-permute-start.3) | collective-permute-done | bytes 131104 | tf_op jit(solution)/shard_map/ppermute | solution.py:264
  19.7 0.0 collective-permute-done.2
  19.8 0.1 broadcast_select_fusion.1
  19.9 29.3 %first_row_sums.1 = (f32[1,4096]{1,0:T(1,128)S(1)}, bf16[128,4096]{1,0:T(8,128)(2,1)S(1)}, f32[1,4096]{1,0:T(1,128)S(1)}, f32[1,3072]{1,0:T(1,128)S(1)}) custom-call(bf16[4,65,768]{2,1,0:T(8,128)(2,1)S(1)} %pad_maximum_fusion.1.t_ref, bf16[16,64,256]{2,1,0:T(8,128)(2,1)S(1)} %pad_maximum_fusion.s_ref.refs_0_), custom_call_target="tpu_custom_call" | custom-call | tf_op jit(solution)/shard_map/first_row_sums/pallas_call | solution.py:210
  49.2 0.0 collective-permute-done.8.t_ref.refs_5_
  49.2 0.0 copy-start.1
  49.3 7.3 %next_row_sums.1 = (f32[1,4096]{1,0:T(1,128)S(1)}, f32[1,3072]{1,0:T(1,128)S(1)}) custom-call(bf16[4,65,768]{2,1,0:T(8,128)(2,1)S(1)} %collective-permute-done.8.t_ref.refs_5_, bf16[128,4096]{1,0:T(8,128)(2,1)S(1)} %get-tuple-element.14.held_ref, f32[1,4096]{1,0:T(1,128)S(1)} %get-tuple-element.15.old_ref, f32[1,4096]{1,0:T(1,128)S(1)} %get-tuple-element.16.prior_ref), custom_call_target="tpu_custom_call" | custom-call | tf_op jit(solution)/shard_map/next_row_sums/pallas_call | solution.py:210
  56.6 0.4 collective-permute-start.11
  57.0 2.2 %collective-permute-start.10 = (f32[1,5120]{1,0:T(1,128)S(1)}, f32[1,5120]{1,0:T(1,128)S(1)}, u32[]{:S(2)}, u32[]{:S(2)}) collective-permute-start(f32[1,5120]{1,0:T(1,128)S(1)} %pad_maximum_fusion.5), channel_id=1, source_target_pairs={{0,96},{32,64},{64,32},{96,0},{1,97},{33,65},{65,33},{97,1},{2,98}... | collective-permute-start | bytes 61448 | tf_op jit(solution)/shard_map/ppermute | solution.py:264
  59.2 1.7 %collective-permute-start.9 = (f32[1,5120]{1,0:T(1,128)S(1)}, f32[1,5120]{1,0:T(1,128)S(1)}, u32[]{:S(2)}, u32[]{:S(2)}) collective-permute-start(f32[1,5120]{1,0:T(1,128)S(1)} %pad_maximum_fusion.5), channel_id=1, source_target_pairs={{0,64},{32,96},{64,0},{96,32},{1,65},{33,97},{65,1},{97,33},{2,66}... | collective-permute-start | bytes 61448 | tf_op jit(solution)/shard_map/ppermute | solution.py:264
  61.0 1.1 collective-permute-done.10
  62.1 2.4 %collective-permute-done.9 = f32[1,5120]{1,0:T(1,128)S(1)} collective-permute-done((f32[1,5120]{1,0:T(1,128)S(1)}, f32[1,5120]{1,0:T(1,128)S(1)}, u32[]{:S(2)}, u32[]{:S(2)}) %collective-permute-start.9) | collective-permute-done | bytes 20512 | tf_op jit(solution)/shard_map/ppermute | solution.py:264
  64.5 0.2 multiply_add_fusion.1
  64.7 0.1 collective-permute-start.13
  64.8 0.1 collective-permute-start.14
  64.9 2.0 %collective-permute-start.12 = (f32[1,4096]{1,0:T(1,128)S(1)}, f32[1,4096]{1,0:T(1,128)S(1)}, u32[]{:S(2)}, u32[]{:S(2)}) collective-permute-start(f32[1,4096]{1,0:T(1,128)S(1)} %multiply_add_fusion.1), channel_id=1, source_target_pairs={{0,1},{1,0},{2,3},{3,2},{4,5},{5,4},{6,7},{7,6},{8,9},{9,8},{10,11... | collective-permute-start | bytes 49160 | tf_op jit(solution)/shard_map/ppermute | solution.py:264
  67.0 1.5 %collective-permute-done.13.refs_2_ = f32[1,4096]{1,0:T(1,128)S(1)} collective-permute-done((f32[1,4096]{1,0:T(1,128)S(1)}, f32[1,4096]{1,0:T(1,128)S(1)}, u32[]{:S(2)}, u32[]{:S(2)}) %collective-permute-start.13) | collective-permute-done | bytes 16416 | tf_op jit(solution)/shard_map/ppermute | solution.py:264
  68.5 0.0 collective-permute-done.14.refs_3_
  68.5 0.0 collective-permute-done.12
  68.5 0.2 add_reduce_fusion
  68.7 32.0 %first_column_sums.1 = (f32[1,3072]{1,0:T(1,128)S(1)}, bf16[4096,128]{1,0:T(8,128)(2,1)S(1)}) custom-call(bf16[16,64,256]{2,1,0:T(8,128)(2,1)S(1)} %pad_maximum_fusion.s_ref.refs_0_, f32[1,4096]{1,0:T(1,128)S(1)} %get-tuple-element.27.refs_1_, f32[1,4096]{1,0:T(1,128)S(1)} %collective-permute-done.13.refs_2_, f32[1,4096]{1,0:T(1,128)S(1)} %collective-permute-done.14.refs_3_, ...), custom_call_target="tpu_custom_call" | custom-call | tf_op jit(solution)/shard_map/first_column_sums/pallas_call | solution.py:210
  100.7 1.8 %collective-permute-start.15 = (f32[1,3072]{1,0:T(1,128)S(1)}, f32[1,3072]{1,0:T(1,128)S(1)}, u32[]{:S(2)}, u32[]{:S(2)}) collective-permute-start(f32[1,3072]{1,0:T(1,128)S(1)} %get-tuple-element.22), channel_id=1, source_target_pairs={{0,8},{8,0},{16,24},{24,16},{1,9},{9,1},{17,25},{25,17},{2,10},{10... | collective-permute-start | bytes 36872 | tf_op jit(solution)/shard_map/ppermute | solution.py:264
  102.5 16.2 %next_column_sums.4 = f32[1,1536]{1,0:T(1,128)S(1)} custom-call(bf16[4096,128]{1,0:T(8,128)(2,1)S(1)} %get-tuple-element.20.stream_ref, bf16[4,65,768]{2,1,0:T(8,128)(2,1)S(1)} %pad_maximum_fusion.1.t_ref, f32[1,3072]{1,0:T(1,128)S(1)} %get-tuple-element.21.bias_ref), custom_call_target="tpu_custom_call" | custom-call | tf_op jit(solution)/shard_map/next_column_sums/pallas_call | solution.py:210
  118.7 0.0 collective-permute-done.15
  118.8 2.4 %collective-permute-start.16 = (f32[1,1536]{1,0:T(1,128)S(1)}, f32[1,1536]{1,0:T(1,128)S(1)}, u32[]{:S(2)}, u32[]{:S(2)}) collective-permute-start(f32[1,1536]{1,0:T(1,128)S(1)} %multiply_add_fusion.2), channel_id=1, source_target_pairs={{0,24},{8,16},{16,8},{24,0},{1,25},{9,17},{17,9},{25,1},{2,26},{10... | collective-permute-start | bytes 18440 | tf_op jit(solution)/shard_map/ppermute | solution.py:264
  121.2 0.6 multiply_subtract_fusion.1
  121.8 8.2 %next_column_sums.3 = f32[1,768]{1,0:T(1,128)S(1)} custom-call(bf16[4096,128]{1,0:T(8,128)(2,1)S(1)} %get-tuple-element.20.stream_ref, bf16[4,65,768]{2,1,0:T(8,128)(2,1)S(1)} %pad_maximum_fusion.1.t_ref, f32[1,3072]{1,0:T(1,128)S(1)} %get-tuple-element.21.bias_ref), custom_call_target="tpu_custom_call" | custom-call | tf_op jit(solution)/shard_map/next_column_sums/pallas_call | solution.py:210
  130.0 0.0 collective-permute-done.16
  130.1 2.2 %collective-permute-start.17 = (f32[1,768]{1,0:T(1,128)S(1)}, f32[1,768]{1,0:T(1,128)S(1)}, u32[]{:S(2)}, u32[]{:S(2)}) collective-permute-start(f32[1,768]{1,0:T(1,128)S(1)} %multiply_add_fusion.3), channel_id=1, source_target_pairs={{0,6},{2,4},{4,2},{6,0},{1,7},{3,5},{5,3},{7,1},{8,14},{10,12},{12... | collective-permute-start | bytes 9224 | tf_op jit(solution)/shard_map/ppermute | solution.py:264
  132.3 8.2 %next_column_sums.5 = f32[1,768]{1,0:T(1,128)S(1)} custom-call(bf16[4096,128]{1,0:T(8,128)(2,1)S(1)} %get-tuple-element.20.stream_ref, bf16[4,65,768]{2,1,0:T(8,128)(2,1)S(1)} %pad_maximum_fusion.1.t_ref, f32[1,3072]{1,0:T(1,128)S(1)} %get-tuple-element.21.bias_ref), custom_call_target="tpu_custom_call" | custom-call | tf_op jit(solution)/shard_map/next_column_sums/pallas_call | solution.py:210
  140.6 0.0 collective-permute-done.17
  140.6 0.1 multiply_reduce_fusion.2
  140.7 0.6 multiply_subtract_fusion
  (33 shorter events, 0.4 us)
Async XLA Ops:
  0.6 1.5 %collective-permute-start = (bf16[1,64,256]{2,1,0:T(8,128)(2,1)}, bf16[1,64,256]{2,1,0:T(8,128)(2,1)S(1)}, u32[]{:S(2)}, u32[]{:S(2)}) collective-permute-start(bf16[1,64,256]{2,1,0:T(8,128)(2,1)} %bitcast.13), channel_id=1, source_target_pairs={{0,1},{1,0},{2,3},{3,2},{4,5},{5,4},{6,7},{7,6},{8,9},{9,8},{10,11... | collective-permute-start | bytes 98312 | tf_op jit(solution)/shard_map/ppermute | solution.py:264
  0.7 0.8 copy-start.2
  0.7 2.9 %copy-start = (bf16[64,768]{1,0:T(8,128)(2,1)S(1)}, bf16[64,768]{1,0:T(8,128)(2,1)}, u32[]{:S(2)}) copy-start(bf16[64,768]{1,0:T(8,128)(2,1)} %param.6) | copy-start | bytes 294916
  1.5 2.1 %copy-start.4 = (bf16[1,768]{1,0:T(2,128)(2,1)S(1)}, bf16[1,768]{1,0:T(2,128)(2,1)}, u32[]{:S(2)}) copy-start(bf16[1,768]{1,0:T(2,128)(2,1)} %param.9) | copy-start | bytes 4612
  2.1 6.3 %collective-permute-start.1 = (bf16[2,64,256]{2,1,0:T(8,128)(2,1)S(1)}, bf16[2,64,256]{2,1,0:T(8,128)(2,1)S(1)}, u32[]{:S(2)}, u32[]{:S(2)}) collective-permute-start(bf16[2,64,256]{2,1,0:T(8,128)(2,1)S(1)} %constant_dynamic-update-slice_fusion), channel_id=1, source_target_pairs={{0,2},{2,0},{4,6},{6,4},{1,3},{3,1},{5,7},{7,5},{8,10},{10,8},{12,... | collective-permute-start | bytes 196616 | tf_op jit(solution)/shard_map/ppermute | solution.py:264
  3.6 9.0 %collective-permute-start.7 = (bf16[1,65,768]{2,1,0:T(8,128)(2,1)S(1)}, bf16[1,65,768]{2,1,0:T(8,128)(2,1)S(1)}, u32[]{:S(2)}, u32[]{:S(2)}) collective-permute-start(bf16[1,65,768]{2,1,0:T(8,128)(2,1)S(1)} %maximum_bitcast_fusion), channel_id=1, source_target_pairs={{0,30},{2,28},{4,26},{6,24},{8,22},{10,20},{12,18},{14,16},{16,14}... | collective-permute-start | bytes 299528 | tf_op jit(solution)/shard_map/ppermute | solution.py:264
  6.8 6.8 %collective-permute-start.6 = (bf16[1,65,768]{2,1,0:T(8,128)(2,1)S(1)}, bf16[1,65,768]{2,1,0:T(8,128)(2,1)S(1)}, u32[]{:S(2)}, u32[]{:S(2)}) collective-permute-start(bf16[1,65,768]{2,1,0:T(8,128)(2,1)S(1)} %maximum_bitcast_fusion), channel_id=1, source_target_pairs={{0,24},{8,16},{16,8},{24,0},{1,25},{9,17},{17,9},{25,1},{2,26},{10... | collective-permute-start | bytes 299528 | tf_op jit(solution)/shard_map/ppermute | solution.py:264
  7.3 6.4 %collective-permute-start.5 = (bf16[1,65,768]{2,1,0:T(8,128)(2,1)S(1)}, bf16[1,65,768]{2,1,0:T(8,128)(2,1)S(1)}, u32[]{:S(2)}, u32[]{:S(2)}) collective-permute-start(bf16[1,65,768]{2,1,0:T(8,128)(2,1)S(1)} %maximum_bitcast_fusion), channel_id=1, source_target_pairs={{0,6},{2,4},{4,2},{6,0},{1,7},{3,5},{5,3},{7,1},{8,14},{10,12},{12... | collective-permute-start | bytes 299528 | tf_op jit(solution)/shard_map/ppermute | solution.py:264
  8.4 4.2 %copy-start.3 = (f32[768]{0:T(1024)S(1)}, f32[768]{0:T(1024)}, u32[]{:S(2)}) copy-start(f32[768]{0:T(1024)} %param.8) | copy-start | bytes 9220
  8.5 8.9 %collective-permute-start.4 = (bf16[4,64,256]{2,1,0:T(8,128)(2,1)S(1)}, bf16[4,64,256]{2,1,0:T(8,128)(2,1)S(1)}, u32[]{:S(2)}, u32[]{:S(2)}) collective-permute-start(bf16[4,64,256]{2,1,0:T(8,128)(2,1)S(1)} %pad_maximum_fusion.4), channel_id=1, source_target_pairs={{0,96},{32,64},{64,32},{96,0},{1,97},{33,65},{65,33},{97,1},{2,98}... | collective-permute-start | bytes 393224 | tf_op jit(solution)/shard_map/ppermute | solution.py:264
  12.6 7.1 %collective-permute-start.3 = (bf16[4,64,256]{2,1,0:T(8,128)(2,1)S(1)}, bf16[4,64,256]{2,1,0:T(8,128)(2,1)S(1)}, u32[]{:S(2)}, u32[]{:S(2)}) collective-permute-start(bf16[4,64,256]{2,1,0:T(8,128)(2,1)S(1)} %pad_maximum_fusion.4), channel_id=1, source_target_pairs={{0,64},{32,96},{64,0},{96,32},{1,65},{33,97},{65,1},{97,33},{2,66}... | collective-permute-start | bytes 393224 | tf_op jit(solution)/shard_map/ppermute | solution.py:264
  12.6 7.1 %collective-permute-start.2 = (bf16[4,64,256]{2,1,0:T(8,128)(2,1)S(1)}, bf16[4,64,256]{2,1,0:T(8,128)(2,1)S(1)}, u32[]{:S(2)}, u32[]{:S(2)}) collective-permute-start(bf16[4,64,256]{2,1,0:T(8,128)(2,1)S(1)} %pad_maximum_fusion.4), channel_id=1, source_target_pairs={{0,32},{32,0},{64,96},{96,64},{1,33},{33,1},{65,97},{97,65},{2,34}... | collective-permute-start | bytes 393224 | tf_op jit(solution)/shard_map/ppermute | solution.py:264
  13.7 35.5 %collective-permute-start.8 = (bf16[4,65,768]{2,1,0:T(8,128)(2,1)S(1)}, bf16[4,65,768]{2,1,0:T(8,128)(2,1)S(1)}, u32[]{:S(2)}, u32[]{:S(2)}) collective-permute-start(bf16[4,65,768]{2,1,0:T(8,128)(2,1)S(1)} %pad_maximum_fusion.1.t_ref), channel_id=1, source_target_pairs={{0,8},{8,0},{16,24},{24,16},{1,9},{9,1},{17,25},{25,17},{2,10},{10... | collective-permute-start | bytes 1198088 | tf_op jit(solution)/shard_map/ppermute | solution.py:264
  49.2 7.4 %copy-start.1 = (f32[1024]{0:T(1024)S(1)}, f32[1024]{0:T(1024)}, u32[]{:S(2)}) copy-start(f32[1024]{0:T(1024)} %param.7) | copy-start | bytes 12292
  56.6 4.4 %collective-permute-start.11 = (f32[1,5120]{1,0:T(1,128)S(1)}, f32[1,5120]{1,0:T(1,128)S(1)}, u32[]{:S(2)}, u32[]{:S(2)}) collective-permute-start(f32[1,5120]{1,0:T(1,128)S(1)} %pad_maximum_fusion.5), channel_id=1, source_target_pairs={{0,32},{32,0},{64,96},{96,64},{1,33},{33,1},{65,97},{97,65},{2,34}... | collective-permute-start | bytes 61448 | tf_op jit(solution)/shard_map/ppermute | solution.py:264
  57.0 5.1 %collective-permute-start.10 = (f32[1,5120]{1,0:T(1,128)S(1)}, f32[1,5120]{1,0:T(1,128)S(1)}, u32[]{:S(2)}, u32[]{:S(2)}) collective-permute-start(f32[1,5120]{1,0:T(1,128)S(1)} %pad_maximum_fusion.5), channel_id=1, source_target_pairs={{0,96},{32,64},{64,32},{96,0},{1,97},{33,65},{65,33},{97,1},{2,98}... | collective-permute-start | bytes 61448 | tf_op jit(solution)/shard_map/ppermute | solution.py:264
  59.2 5.3 %collective-permute-start.9 = (f32[1,5120]{1,0:T(1,128)S(1)}, f32[1,5120]{1,0:T(1,128)S(1)}, u32[]{:S(2)}, u32[]{:S(2)}) collective-permute-start(f32[1,5120]{1,0:T(1,128)S(1)} %pad_maximum_fusion.5), channel_id=1, source_target_pairs={{0,64},{32,96},{64,0},{96,32},{1,65},{33,97},{65,1},{97,33},{2,66}... | collective-permute-start | bytes 61448 | tf_op jit(solution)/shard_map/ppermute | solution.py:264
  64.7 3.8 %collective-permute-start.13 = (f32[1,4096]{1,0:T(1,128)S(1)}, f32[1,4096]{1,0:T(1,128)S(1)}, u32[]{:S(2)}, u32[]{:S(2)}) collective-permute-start(f32[1,4096]{1,0:T(1,128)S(1)} %multiply_add_fusion.1), channel_id=1, source_target_pairs={{0,2},{2,0},{4,6},{6,4},{1,3},{3,1},{5,7},{7,5},{8,10},{10,8},{12,... | collective-permute-start | bytes 49160 | tf_op jit(solution)/shard_map/ppermute | solution.py:264
  64.8 3.7 %collective-permute-start.14 = (f32[1,4096]{1,0:T(1,128)S(1)}, f32[1,4096]{1,0:T(1,128)S(1)}, u32[]{:S(2)}, u32[]{:S(2)}) collective-permute-start(f32[1,4096]{1,0:T(1,128)S(1)} %multiply_add_fusion.1), channel_id=1, source_target_pairs={{0,3},{1,2},{2,1},{3,0},{4,7},{5,6},{6,5},{7,4},{8,11},{9,10},{10,... | collective-permute-start | bytes 49160 | tf_op jit(solution)/shard_map/ppermute | solution.py:264
  64.9 3.6 %collective-permute-start.12 = (f32[1,4096]{1,0:T(1,128)S(1)}, f32[1,4096]{1,0:T(1,128)S(1)}, u32[]{:S(2)}, u32[]{:S(2)}) collective-permute-start(f32[1,4096]{1,0:T(1,128)S(1)} %multiply_add_fusion.1), channel_id=1, source_target_pairs={{0,1},{1,0},{2,3},{3,2},{4,5},{5,4},{6,7},{7,6},{8,9},{9,8},{10,11... | collective-permute-start | bytes 49160 | tf_op jit(solution)/shard_map/ppermute | solution.py:264
  100.7 18.0 %collective-permute-start.15 = (f32[1,3072]{1,0:T(1,128)S(1)}, f32[1,3072]{1,0:T(1,128)S(1)}, u32[]{:S(2)}, u32[]{:S(2)}) collective-permute-start(f32[1,3072]{1,0:T(1,128)S(1)} %get-tuple-element.22), channel_id=1, source_target_pairs={{0,8},{8,0},{16,24},{24,16},{1,9},{9,1},{17,25},{25,17},{2,10},{10... | collective-permute-start | bytes 36872 | tf_op jit(solution)/shard_map/ppermute | solution.py:264
  118.8 11.3 %collective-permute-start.16 = (f32[1,1536]{1,0:T(1,128)S(1)}, f32[1,1536]{1,0:T(1,128)S(1)}, u32[]{:S(2)}, u32[]{:S(2)}) collective-permute-start(f32[1,1536]{1,0:T(1,128)S(1)} %multiply_add_fusion.2), channel_id=1, source_target_pairs={{0,24},{8,16},{16,8},{24,0},{1,25},{9,17},{17,9},{25,1},{2,26},{10... | collective-permute-start | bytes 18440 | tf_op jit(solution)/shard_map/ppermute | solution.py:264
  130.1 10.5 %collective-permute-start.17 = (f32[1,768]{1,0:T(1,128)S(1)}, f32[1,768]{1,0:T(1,128)S(1)}, u32[]{:S(2)}, u32[]{:S(2)}) collective-permute-start(f32[1,768]{1,0:T(1,128)S(1)} %multiply_add_fusion.3), channel_id=1, source_target_pairs={{0,6},{2,4},{4,2},{6,0},{1,7},{3,5},{5,3},{7,1},{8,14},{10,12},{12... | collective-permute-start | bytes 9224 | tf_op jit(solution)/shard_map/ppermute | solution.py:264
